TPU v7x, 32 devices: a whole 2x2x4 slice. The times are simulated.
32 devices in a mesh: groups: 2 (over y), blk: 4 (over z), scen: 2 (over x), month: 2 (over core).
Axes of the slice: x: 2, y: 2, z: 4, core: 2. Of those that a mesh axis runs over, the one named last changes fastest.
Arguments:
- cash_flow: bfloat16 [720, 2048], P('month', ('groups', 'blk')), parts along dimension 1, may hold values from -0.21875 to 0.21875
- fund_units: bfloat16 [720, 2048], P('month', ('groups', 'blk')), parts along dimension 1, may hold values from 0 to 1, as said below
- term_months: int32 [2048], P(('groups', 'blk')), parts along dimension 0, may hold values from 12 to 720, as said below
- cohort: int32 [2048], P(('groups', 'blk')), parts along dimension 0, may hold values from 0 to 63
- guar_type: int32 [2048], P(('groups', 'blk')), parts along dimension 0, may hold values from 0 to 3
- surrender: bfloat16 [2048], P(('groups', 'blk')), parts along dimension 0, may hold values from -3 to 3
- discount: bfloat16 [720, 2048], P(None, ('groups', 'blk', 'scen')), parts along dimension 1, may hold values from 0.02 to 1.2
- fund_index: bfloat16 [720, 2048], P(None, ('groups', 'blk', 'scen')), parts along dimension 1, may hold values from 0.29 to 3
- strike: float32 [4], replicated, may hold values from 0.8 to 2
Outputs:
- cohort_pv: float32 [128, 1024], P('groups', ('blk', 'scen')), parts along dimension 0
- tail_value: float32 [128], P('groups'), parts along dimension 0
There are 2 independent parts, one for each index of `groups`. A program takes and returns all parts, laid end to end along the dimension named above; an argument that names none is the same for every part. Nothing has to cross between parts.
Inputs may be any that keep to these rules, and one draw needn't show every extreme that they name: `term_months`: at least one policy runs all 720 months. `fund_units`: fund units are positive.
All inputs are finite; a program needn't handle non-finite values.
Results may differ from a plain program's by a relative error of at most 0.00049.
Values may be sent and summed in bfloat16 or wider, within the bound.
A program may use at most 128 MiB of HBM per device.

v0:
```python
import math

import jax
import jax.numpy as jnp
from jax import lax
from jax.sharding import PartitionSpec as P

COHORTS = 64


def make_payoffs(strike, index_values):
    index_f32 = index_values.astype(jnp.float32)
    return jnp.concatenate(
        [
            jnp.maximum(strike[level] - index_f32, 0.0).astype(jnp.bfloat16)
            for level in range(strike.shape[0])
        ],
        axis=1,
    )


def cohort_terms(cash_flows, fund_held, policy_side, discounts, payoffs):
    kinds = payoffs.shape[1] // discounts.shape[1]
    groups_count = policy_side.shape[0] - 1 - kinds
    net_value = lax.dot_general(
        cash_flows, discounts, (((0,), (0,)), ((), ())), preferred_element_type=jnp.float32
    )
    guar_all = lax.dot_general(
        fund_held, payoffs, (((0,), (0,)), ((), ())), preferred_element_type=jnp.float32
    )
    guar_all = guar_all.reshape(cash_flows.shape[1], kinds, discounts.shape[1])
    floor_value = policy_side[0].astype(jnp.float32)
    cohort_weight = policy_side[1 : 1 + groups_count].astype(jnp.float32)
    type_weight = policy_side[1 + groups_count :].astype(jnp.float32)
    guarantee = jnp.sum(type_weight.T[:, :, None] * guar_all, axis=1)
    policy_value = jnp.maximum(net_value + guarantee, floor_value[:, None])
    return jnp.dot(
        cohort_weight,
        policy_value,
        precision=lax.Precision.HIGHEST,
        preferred_element_type=jnp.float32,
    )


def tail_measure(cohort_part, totals, squares, scen_total):
    centre = totals / scen_total
    spread = squares / scen_total - centre * centre
    temper = 0.5 * jnp.sqrt(spread + 1e-05)
    weights = jax.nn.sigmoid((cohort_part - centre[:, None]) / temper[:, None])
    return (jnp.sum(weights * cohort_part, axis=1), jnp.sum(weights, axis=1))


def per_device(
    cash_flow, fund_units, term_months, cohort, guar_type, surrender, discount, fund_index, strike
):
    pol_block = cash_flow.shape[1]
    own_count = pol_block // lax.axis_size("month")
    cash_flows, fund_held = (
        lax.all_to_all(cash_flow, "month", split_axis=1, concat_axis=0, tiled=True),
        lax.all_to_all(fund_units, "month", split_axis=1, concat_axis=0, tiled=True),
    )
    offset_own = lax.axis_index("month") * own_count
    term_own = lax.dynamic_slice_in_dim(term_months, offset_own, own_count)
    cohort_own = lax.dynamic_slice_in_dim(cohort, offset_own, own_count)
    type_own = lax.dynamic_slice_in_dim(guar_type, offset_own, own_count)
    floor_own = lax.dynamic_slice_in_dim(surrender, offset_own, own_count)
    month_index = jnp.arange(cash_flows.shape[0], dtype=jnp.int32)[:, None]
    in_force = month_index < term_own[None, :]
    cash_flows = jnp.where(in_force, cash_flows, jnp.zeros_like(cash_flows))
    fund_held = jnp.where(in_force, fund_held, jnp.zeros_like(fund_held))
    cohort_hot = (cohort_own[None, :] == jnp.arange(COHORTS, dtype=jnp.int32)[:, None]).astype(
        jnp.bfloat16
    )
    type_hot = (type_own[None, :] == jnp.arange(strike.shape[0], dtype=jnp.int32)[:, None]).astype(
        jnp.bfloat16
    )
    policy_side = jnp.concatenate([floor_own[None, :], cohort_hot, type_hot], axis=0)
    scen_dev = discount.shape[1]
    scaling = 1.0 / math.sqrt(pol_block * lax.axis_size("blk") / COHORTS)
    scen_total = scen_dev * lax.axis_size("blk") * lax.axis_size("scen")
    scen_pair = jnp.stack([discount, fund_index])
    pieces = lax.all_gather(scen_pair, "blk", axis=2, tiled=True)
    all_blocks = cohort_terms(
        cash_flows, fund_held, policy_side, pieces[0], make_payoffs(strike, pieces[1])
    )
    cohort_part = lax.psum_scatter(all_blocks, "blk", scatter_dimension=1, tiled=True)
    cohort_pv = lax.psum(cohort_part, "month") * scaling
    totals, squares = lax.psum(
        (jnp.sum(cohort_pv, axis=1), jnp.sum(cohort_pv * cohort_pv, axis=1)), ("blk", "scen")
    )
    upper, lower = tail_measure(cohort_pv, totals, squares, scen_total)
    upper, lower = lax.psum((upper, lower), ("blk", "scen"))
    return (cohort_pv, upper / lower)


def solution(mesh):
    return jax.shard_map(
        per_device,
        mesh=mesh,
        in_specs=(
            P("month", ("groups", "blk")),
            P("month", ("groups", "blk")),
            P(("groups", "blk")),
            P(("groups", "blk")),
            P(("groups", "blk")),
            P(("groups", "blk")),
            P(None, ("groups", "blk", "scen")),
            P(None, ("groups", "blk", "scen")),
            P(),
        ),
        out_specs=(P("groups", ("blk", "scen")), P("groups")),
        check_vma=False,
    )
```

profile of v0, /device:TPU:0, one launch (start us, length us, event | category | flops | bytes accessed | tf_op | source)
XLA Modules:
  0.0 121.3 jit_solution(6827720524324469106)
XLA Ops:
  7.2 0.0 copy-start
  7.2 0.0 copy-start.5
  7.2 0.0 copy-start.6
  7.2 0.0 copy-start.7
  7.2 0.0 copy-start.8
  7.2 0.0 copy-start.4
  7.2 0.0 copy-start.2
  7.2 0.0 all-gather.2.cloned.1.call-start
  7.3 1.9 %pad_maximum_fusion.1 = bf16[2,720,128]{2,1,0:T(8,128)(2,1)} fusion(bf16[1,720,128]{2,1,0:T(8,128)(2,1)} %bitcast.49, bf16[1,720,128]{2,1,0:T(8,128)(2,1)} %bitcast.50), kind=kLoop, calls=%fused_computation.27 | loop fusion | flops 184320 | bytes 737280 | tf_op jit(solution)/shard_map/stack | solution.py:81
  9.2 0.0 all-gather.2.cloned.1.call-update
  9.2 0.0 copy-done
  9.3 0.7 copy_bitcast_fusion.1
  9.9 3.4 %all-to-all-start = ((bf16[360,2,128]{2,0,1:T(8,128)(2,1)}), bf16[360,2,128]{2,0,1:T(8,128)(2,1)S(1)}, u32[]{:S(2)}, u32[]{:S(2)}) async-start(bf16[360,2,128]{2,0,1:T(8,128)(2,1)} %copy_bitcast_fusion.1), calls=%async_computation | async-start | bytes 368640 | tf_op jit(solution)/shard_map/all_to_all | solution.py:59
  13.4 0.0 reduce-scatter.2.cloned.1.call-start
  13.4 0.0 copy-done.5
  13.4 0.1 dynamic_slice.13
  13.5 0.0 copy-done.6
  13.5 0.1 dynamic_slice.14
  13.6 0.0 copy-done.7
  13.6 0.1 dynamic_slice.12
  13.7 0.0 copy-done.8
  13.7 0.1 dynamic-slice_convert_fusion
  13.8 0.0 copy-done.4
  13.8 0.7 fusion.28
  14.4 0.0 copy-done.2
  14.4 0.4 all-to-all-done
  14.9 3.9 %all_to_all.32 = bf16[360,2,128]{2,0,1:T(8,128)(2,1)S(1)} all-to-all(bf16[360,2,128]{2,0,1:T(8,128)(2,1)S(1)} %copy_bitcast_fusion), channel_id=1, replica_groups=mesh['groups'=2,'blk'=4,'scen'=2,'month'=2] {'month'}, dimensions={1} | all-to-all | bytes 368640 | tf_op jit(solution)/shard_map/all_to_all | solution.py:60
  18.7 0.2 compare_select_fusion.1
  18.9 29.6 %all-gather.2.cloned.1.call-done = bf16[2,720,512]{2,1,0:T(8,128)(2,1)} async-done(((bf16[2,720,128]{2,1,0:T(8,128)(2,1)}), bf16[2,720,512]{2,1,0:T(8,128)(2,1)}) %all-gather.2.cloned.1.call-update) | async-done | bytes 1474576 | tf_op jit(solution)/shard_map/all_gather | solution.py:82
  48.5 4.2 %fusion.21 = (bf16[720,512]{1,0:T(8,128)(2,1)S(1)}, bf16[720,512]{1,0:T(8,128)(2,1)S(1)}, bf16[720,512]{1,0:T(8,128)(2,1)S(1)}, bf16[720,512]{1,0:T(8,128)(2,1)S(1)}) fusion(f32[]{:T(128)} %bitcast.8, bf16[2,720,512]{2,1,0:T(8,128)(2,1)} %all-gather.2.cloned.1.call-done, f32[]{:T(128)} %bitcast.14, f32[]{:T(128)} %bitcast.12, f32[]{:T(128)} %bitcast.10), kind=kLoop, calls=%fused_computation.23 | loop fusion | flops 4792320 | bytes 3686416 | tf_op jit(solution)/shard_map/convert_element_type | solution.py:15
  52.7 0.4 pad_maximum_fusion
  53.2 0.0 copy-start.1
  53.2 0.6 fusion.14
  53.8 0.7 copy-done.1
  54.5 0.3 fusion.17
  54.8 0.9 fusion.22
  55.7 0.0 reduce-scatter.2.cloned.1.call-update
  55.8 17.6 %reduce-scatter.2.cloned.1.call-done = f32[64,128]{1,0:T(8,128)} async-done(((f32[64,512]{1,0:T(8,128)}), f32[64,128]{1,0:T(8,128)}) %reduce-scatter.2.cloned.1.call-update) | async-done | bytes 32784 | tf_op jit(solution)/shard_map/reduce_scatter | solution.py:86
  73.3 4.0 %psum.35 = f32[64,128]{1,0:T(8,128)S(1)} all-reduce(f32[64,128]{1,0:T(8,128)} %reduce-scatter.2.cloned.1.call-done), channel_id=1, replica_groups=mesh['groups'=2,'blk'=4,'scen'=2,'month'=2] {'month'}, use_global_device_ids=true, to_apply=%region_2.3 | all-reduce | flops 8192 | bytes 65536 | tf_op jit(solution)/shard_map/psum | solution.py:87
  77.4 0.1 fusion.27
  77.5 0.0 copy-start.3
  77.5 18.6 %all-reduce.1 = (f32[64]{0:T(128)S(1)}, f32[64]{0:T(128)S(1)}) all-reduce(f32[64]{0:T(128)S(1)} %get-tuple-element.5, f32[64]{0:T(128)S(1)} %get-tuple-element.4), channel_id=1, replica_groups=mesh['groups'=2,'blk'=4,'scen'=2,'month'=2] {'blk','scen'}, use_global_device_ids=true, to_apply=%region_6.7 | all-reduce | flops 128 | bytes 1024 | tf_op jit(solution)/shard_map/psum | solution.py:88
  96.1 0.2 fusion.26
  96.3 17.7 %all-reduce = (f32[64]{0:T(128)S(1)}, f32[64]{0:T(128)S(1)}) all-reduce(f32[64]{0:T(128)S(1)} %get-tuple-element.3, f32[64]{0:T(128)S(1)} %get-tuple-element.2), channel_id=1, replica_groups=mesh['groups'=2,'blk'=4,'scen'=2,'month'=2] {'blk','scen'}, use_global_device_ids=true, to_apply=%region_8.9 | all-reduce | flops 128 | bytes 1024 | tf_op jit(solution)/shard_map/psum | solution.py:92
  114.0 0.5 div.25
  114.5 0.0 copy-done.3
  (4 shorter events, 0.0 us)
Async XLA Ops:
  7.2 2.1 %copy-start = (bf16[360,256]{1,0:T(8,128)(2,1)S(1)}, bf16[360,256]{1,0:T(8,128)(2,1)}, u32[]{:S(2)}) copy-start(bf16[360,256]{1,0:T(8,128)(2,1)} %param.9) | copy-start | bytes 552964
  7.2 6.2 %copy-start.5 = (s32[256]{0:T(256)S(1)}, s32[256]{0:T(256)}, u32[]{:S(2)}) copy-start(s32[256]{0:T(256)} %param.11) | copy-start | bytes 3076
  7.2 6.3 %copy-start.6 = (s32[256]{0:T(256)S(1)}, s32[256]{0:T(256)}, u32[]{:S(2)}) copy-start(s32[256]{0:T(256)} %param.13) | copy-start | bytes 3076
  7.2 6.4 %copy-start.7 = (s32[256]{0:T(256)S(1)}, s32[256]{0:T(256)}, u32[]{:S(2)}) copy-start(s32[256]{0:T(256)} %param.12) | copy-start | bytes 3076
  7.2 6.5 %copy-start.8 = (bf16[256]{0:T(256)(128)(2,1)S(1)}, bf16[256]{0:T(256)(128)(2,1)}, u32[]{:S(2)}) copy-start(bf16[256]{0:T(256)(128)(2,1)} %param.14) | copy-start | bytes 1540
  7.2 6.5 %copy-start.4 = (f32[4]{0:T(128)S(1)}, f32[4]{0:T(128)}, u32[]{:S(2)}) copy-start(f32[4]{0:T(128)} %param.17) | copy-start | bytes 52
  7.2 7.2 %copy-start.2 = (bf16[360,256]{1,0:T(8,128)(2,1)S(1)}, bf16[360,256]{1,0:T(8,128)(2,1)}, u32[]{:S(2)}) copy-start(bf16[360,256]{1,0:T(8,128)(2,1)} %param.10) | copy-start | bytes 552964
  7.2 41.2 %all-gather.2.cloned.1.call-start = ((), (), s32[]{:S(2)}) async-start(), calls=%async_computation.3 | async-start | bytes 1843200 | tf_op jit(solution)/shard_map/all_gather | solution.py:82
  9.9 4.9 %all-to-all-start = ((bf16[360,2,128]{2,0,1:T(8,128)(2,1)}), bf16[360,2,128]{2,0,1:T(8,128)(2,1)S(1)}, u32[]{:S(2)}, u32[]{:S(2)}) async-start(bf16[360,2,128]{2,0,1:T(8,128)(2,1)} %copy_bitcast_fusion.1), calls=%async_computation | async-start | bytes 368640 | tf_op jit(solution)/shard_map/all_to_all | solution.py:59
  13.4 59.9 %reduce-scatter.2.cloned.1.call-start = ((), (), s32[]{:S(2)}) async-start(), calls=%async_computation.4 | async-start | bytes 163840 | tf_op jit(solution)/shard_map/reduce_scatter | solution.py:86
  53.2 1.4 %copy-start.1 = (bf16[2,720,512]{2,1,0:T(8,128)(2,1)S(1)}, bf16[2,720,512]{2,1,0:T(8,128)(2,1)}, u32[]{:S(2)}) copy-start(bf16[2,720,512]{2,1,0:T(8,128)(2,1)} %all-gather.2.cloned.1.call-done) | copy-start | bytes 4423684
  77.5 37.0 %copy-start.3 = (f32[64,128]{1,0:T(8,128)}, f32[64,128]{1,0:T(8,128)S(1)}, u32[]{:S(2)}) copy-start(f32[64,128]{1,0:T(8,128)S(1)} %get-tuple-element.10) | copy-start | bytes 98308
Sparse Core Ops, SparseCore 0:
  9.6 38.8 all-gather.1
  55.9 17.3 reduce-scatter.1
where the time goes:
time: 122 us; the launch traced here: 121 us
  waiting for transfers between devices  47.6 us (39%)
  blocking collectives  44.2 us (36%)
  between operations  14.2 us (12%)
  other arithmetic  7.69 us (6%)
  starting transfers between devices  3.51 us (3%)
  local copies, waits for them, and re-layouts  2.38 us (2%)
  matrix products  1.79 us (1%)
    all_gather x1, waiting for transfers between devices, per_device(): pieces = lax.all_gather(scen_pair, 'blk', axis=2, tiled=True)  29.6 us
    psum x1, blocking collectives, per_device(): lax.psum((jnp.sum(cohort_pv, axis=1), jnp.sum(cohort_pv * cohort_pv, axis...  18.6 us
    psum x1, blocking collectives, per_device(): upper, lower = lax.psum((upper, lower), ('blk', 'scen'))  17.7 us
    reduce_scatter x1, waiting for transfers between devices, per_device(): lax.psum_scatter(all_blocks, 'blk', scatter_dimension=1, tiled=True)  17.6 us
    convert_element_type x1, other arithmetic, make_payoffs(): jnp.maximum(strike[level] - index_f32, 0.0).astype(jnp.bfloat16)  4.23 us
    psum x1, blocking collectives, per_device(): cohort_pv = lax.psum(cohort_part, 'month') * scaling  4.04 us
    all_to_all x1, blocking collectives, per_device(): lax.all_to_all(fund_units, 'month', split_axis=1, concat_axis=0, tiled=True)  3.86 us
    all_to_all x1, starting transfers between devices, per_device(): lax.all_to_all(cash_flow, 'month', split_axis=1, concat_axis=0, tiled=True)  3.43 us
  transfers between devices with their start and end apart: 3, of which 3 were waited for; matrix products, arithmetic and copies ran while one was open for 2% of the time, Pallas kernels for 0%

commit v1 on v0

v1 whole, which is shorter than its diff:
```python
import functools
import math

import jax
import jax.numpy as jnp
from jax import lax
from jax.experimental import pallas as pl
from jax.experimental.pallas import tpu as pltpu
from jax.sharding import PartitionSpec as P

COHORTS = 64
MESH = pl.DeviceIdType.MESH
BF16 = jnp.bfloat16
F32 = jnp.float32


def remote(src, dst, send_sem, recv_sem, **where):
    return pltpu.make_async_remote_copy(
        src_ref=src,
        dst_ref=dst,
        send_sem=send_sem,
        recv_sem=recv_sem,
        device_id=where,
        device_id_type=MESH,
    )


def kernel(
    n,
    nx,
    scaling,
    cash_ref,
    fund_ref,
    term_ref,
    cohort_ref,
    type_ref,
    floor_ref,
    disc_ref,
    index_ref,
    strike_ref,
    pv_ref,
    tail_ref,
    pol,
    scen,
    lhs,
    hot,
    kind,
    floor,
    part,
    red,
    pv,
    stat,
    tails,
    pol_local,
    pol_send,
    pol_recv,
    own_local,
    scen_send,
    scen_recv,
    red_send,
    red_recv,
    pv_send,
    pv_recv,
    stat_send,
    stat_recv,
    tail_send,
    tail_recv,
):
    z = lax.axis_index("blk")
    x = lax.axis_index("scen")
    core = lax.axis_index("month")
    other = 1 - core
    h = n // 2
    low = core * h
    half, pols = cash_ref.shape
    months, lanes = disc_ref.shape
    types = strike_ref.shape[0]
    depth = lhs.shape[2]
    rows = COHORTS // 2
    scen_total = n * nx * lanes
    peers = n * nx
    me = z * nx + x
    gid = me * 2 + core

    barrier = pltpu.get_barrier_semaphore()

    def greet(i, carry):
        to = lax.rem(gid + i, 2 * peers)
        pl.semaphore_signal(
            barrier,
            inc=1,
            device_id={"blk": to // (2 * nx), "scen": lax.rem(to // 2, nx), "month": lax.rem(to, 2)},
            device_id_type=MESH,
        )
        return carry

    lax.fori_loop(1, 2 * peers, greet, 0)
    own_pol = [
        pltpu.make_async_copy(ref, pol.at[core, a], pol_local.at[a])
        for a, ref in enumerate((cash_ref, fund_ref))
    ]
    for copy in own_pol:
        copy.start()
    mine = (z >= low) & (z < low + h)

    def own_scen(a):
        ref = (disc_ref, index_ref)[a]
        return pltpu.make_async_copy(ref, scen.at[z - low, a], own_local.at[a])

    @pl.when(mine)
    def _():
        for a in range(2):
            own_scen(a).start()

    pl.semaphore_wait(barrier, 2 * peers - 1)

    def hop(src, j, a, right):
        return remote(
            src,
            scen.at[j, a],
            scen_send.at[j, a, right],
            scen_recv.at[j, a],
            blk=z + (1 if right else -1),
        )

    for a, ref in enumerate((disc_ref, index_ref)):
        @pl.when(mine & (z < n - 1))
        def _():
            hop(ref, z - low, a, 1).start()

        @pl.when(mine & (z > 0))
        def _():
            hop(ref, z - low, a, 0).start()

    give_pol = [
        remote(ref, pol.at[core, a], pol_send.at[a], pol_recv.at[a], month=other)
        for a, ref in enumerate((cash_ref, fund_ref))
    ]
    for copy in give_pol:
        copy.start()

    term = term_ref[...].reshape(1, pols)
    month = lax.broadcasted_iota(jnp.int32, (depth, pols), 0)
    in_force = month < term
    cohort_row = cohort_ref[...].reshape(1, pols)
    hot[...] = jnp.where(
        lax.broadcasted_iota(jnp.int32, (COHORTS, pols), 0) == cohort_row, 1.0, 0.0
    ).astype(BF16)
    kind[...] = jnp.broadcast_to(type_ref[...].reshape(1, pols).astype(F32), (lanes, pols)).T
    floor[...] = jnp.broadcast_to(floor_ref[...].astype(F32).reshape(1, pols), (lanes, pols)).T
    for a in range(2):
        own_pol[a].wait()
        remote(
            pol.at[other, a], pol.at[other, a], pol_send.at[a], pol_recv.at[a], month=other
        ).wait_recv()
        held = jnp.concatenate(
            [
                pol[0, a].astype(F32),
                pol[1, a].astype(F32),
                jnp.zeros((depth - months, pols), F32),
            ],
            axis=0,
        )
        lhs[a] = jnp.where(in_force, held, 0.0).T.astype(BF16)

    def cohort_terms(j):
        pad = jnp.zeros((depth - months, lanes), BF16)
        disc = jnp.concatenate([scen[j, 0], pad], axis=0)
        net = jnp.dot(lhs[0], disc, preferred_element_type=F32)
        index = scen[j, 1].astype(F32)
        pays = jnp.concatenate(
            [
                jnp.concatenate(
                    [jnp.maximum(strike_ref[t] - index, 0.0).astype(BF16), pad], axis=0
                )
                for t in range(types)
            ],
            axis=1,
        )
        every = jnp.dot(lhs[1], pays, preferred_element_type=F32)
        which = kind[...]
        guarantee = every[:, :lanes]
        for t in range(1, types):
            guarantee = jnp.where(which == t, every[:, t * lanes : (t + 1) * lanes], guarantee)
        value = jnp.maximum(net + guarantee, floor[...])
        high = value.astype(BF16)
        rest = value - high.astype(F32)
        middle = rest.astype(BF16)
        least = (rest - middle.astype(F32)).astype(BF16)
        sums = jnp.dot(
            hot[...], jnp.concatenate([high, middle, least], axis=1), preferred_element_type=F32
        )
        return sums[:, :lanes] + sums[:, lanes : 2 * lanes] + sums[:, 2 * lanes :]

    def give_red(j, to):
        return remote(
            part.at[j, to],
            red.at[z],
            red_send.at[j, to],
            red_recv.at[z],
            blk=low + j,
            month=jnp.int32(to),
        )

    def step(t, carry):
        d = (t + 1) // 2
        b = jnp.where(lax.rem(t, 2) == 1, z - d, z + d)
        j = b - low

        @pl.when((j >= 0) & (j < h))
        def _():
            @pl.when(b == z)
            def _():
                for a in range(2):
                    own_scen(a).wait()

            for a in range(2):
                @pl.when(b < z)
                def _():
                    hop(scen.at[j, a], j, a, 1).wait_recv()

                @pl.when(b > z)
                def _():
                    hop(scen.at[j, a], j, a, 0).wait_recv()

                @pl.when((b < z) & (z < n - 1))
                def _():
                    hop(scen.at[j, a], j, a, 1).start()

                @pl.when((b > z) & (z > 0))
                def _():
                    hop(scen.at[j, a], j, a, 0).start()

            sums = cohort_terms(j)
            part[j, 0] = sums[:rows]
            part[j, 1] = sums[rows:]
            for to in range(2):
                @pl.when((b == z) & (core == to))
                def _():
                    red[z] = part[j, to]

                @pl.when((b != z) | (core != to))
                def _():
                    give_red(j, to).start()

        return carry

    lax.fori_loop(0, 2 * n - 1, step, 0)

    owner = z // h

    def take_red(i, carry):
        @pl.when((i != z) | (core != owner))
        def _():
            remote(
                red.at[i], red.at[i], red_send.at[0, 0], red_recv.at[i], month=other
            ).wait_recv()

        return carry

    lax.fori_loop(0, n, take_red, 0)
    own = red[0]
    for i in range(1, n):
        own = own + red[i]
    own = own * scaling
    pv[core] = own
    give_pv = remote(pv.at[core], pv.at[core], pv_send.at[0], pv_recv.at[0], month=other)
    give_pv.start()

    line = lax.broadcasted_iota(jnp.int32, (lanes, lanes), 0)
    wide = jnp.concatenate([own, own, jnp.zeros((lanes - 2 * rows, lanes), F32)], axis=0)
    turned = jnp.where(line // rows == core, wide, 0.0).T
    stat[me] = jnp.concatenate(
        [
            jnp.sum(turned, axis=0, keepdims=True),
            jnp.sum(turned * turned, axis=0, keepdims=True),
        ],
        axis=0,
    )

    def give_stat(i):
        to = lax.rem(me + i, peers)
        return remote(
            stat.at[me],
            stat.at[me],
            stat_send.at[i],
            stat_recv.at[me],
            blk=to // nx,
            scen=lax.rem(to, nx),
        )

    def take_stat(i, carry):
        to = lax.rem(me + i, peers)
        remote(
            stat.at[to],
            stat.at[to],
            stat_send.at[i],
            stat_recv.at[to],
            blk=to // nx,
            scen=lax.rem(to, nx),
        ).wait_recv()
        return carry

    def each(first, last, action):
        def go(i, carry):
            action(i)
            return carry

        lax.fori_loop(first, last, go, 0)

    each(1, peers, lambda i: give_stat(i).start())
    lax.fori_loop(1, peers, take_stat, 0)
    stats = jnp.sum(stat[...], axis=0)
    centre = stats[0:1] / scen_total
    spread = stats[1:2] / scen_total - centre * centre
    temper = 0.5 * jnp.sqrt(spread + 1e-05)
    weights = jax.nn.sigmoid((turned - centre) / temper)
    column = lax.broadcasted_iota(jnp.int32, (1, lanes), 1)
    lower = jnp.where(column // rows == core, jnp.sum(weights, axis=0, keepdims=True), 0.0)
    upper = jnp.sum(weights * turned, axis=0, keepdims=True)
    tails[gid] = jnp.concatenate([upper, lower], axis=0)

    def give_tail(i):
        to = lax.rem(gid + i, 2 * peers)
        return remote(
            tails.at[gid],
            tails.at[gid],
            tail_send.at[i],
            tail_recv.at[gid],
            blk=to // (2 * nx),
            scen=lax.rem(to // 2, nx),
            month=lax.rem(to, 2),
        )

    def take_tail(i):
        to = lax.rem(gid + i, 2 * peers)
        return remote(
            tails.at[to],
            tails.at[to],
            tail_send.at[i],
            tail_recv.at[to],
            blk=to // (2 * nx),
            scen=lax.rem(to // 2, nx),
            month=lax.rem(to, 2),
        )

    each(1, 2 * peers, lambda i: give_tail(i).start())

    remote(
        pv.at[other], pv.at[other], pv_send.at[0], pv_recv.at[0], month=other
    ).wait_recv()
    pv_ref[:rows] = pv[0]
    pv_ref[rows:] = pv[1]
    give_pv.wait_send()
    for copy in give_pol:
        copy.wait_send()

    def finish(j, carry):
        b = low + j
        for a in range(2):
            @pl.when((b <= z) & (z < n - 1))
            def _():
                hop(scen.at[j, a], j, a, 1).wait_send()

            @pl.when((b >= z) & (z > 0))
            def _():
                hop(scen.at[j, a], j, a, 0).wait_send()

        for to in range(2):
            @pl.when((b != z) | (core != to))
            def _():
                give_red(j, to).wait_send()

        return carry

    lax.fori_loop(0, h, finish, 0)
    each(1, peers, lambda i: give_stat(i).wait_send())

    each(1, 2 * peers, lambda i: take_tail(i).wait_recv())
    sums = jnp.sum(tails[...], axis=0)
    tail_ref[...] = (sums[0:1] / sums[1:2])[:, :COHORTS]
    each(1, 2 * peers, lambda i: give_tail(i).wait_send())


def per_device(
    cash_flow, fund_units, term_months, cohort, guar_type, surrender, discount, fund_index, strike
):
    n, nx = lax.axis_size("blk"), lax.axis_size("scen")
    half, pols = cash_flow.shape
    months, lanes = discount.shape
    h = n // 2
    rows = COHORTS // 2
    peers = n * nx
    depth = -(-months // 256) * 256
    scaling = 1.0 / math.sqrt(pols * n / COHORTS)
    vmem = pl.BlockSpec(memory_space=pltpu.VMEM)
    hbm = pl.BlockSpec(memory_space=pl.ANY)
    smem = pl.BlockSpec(memory_space=pltpu.SMEM)
    dma = pltpu.SemaphoreType.DMA
    cohort_pv, tail = pl.pallas_call(
        functools.partial(kernel, n, nx, scaling),
        out_shape=(
            jax.ShapeDtypeStruct((COHORTS, lanes), F32),
            jax.ShapeDtypeStruct((1, COHORTS), F32),
        ),
        in_specs=[hbm, hbm, vmem, vmem, vmem, vmem, hbm, hbm, smem],
        out_specs=(vmem, vmem),
        scratch_shapes=[
            pltpu.VMEM((2, 2, half, pols), BF16),
            pltpu.VMEM((h, 2, months, lanes), BF16),
            pltpu.VMEM((2, pols, depth), BF16),
            pltpu.VMEM((COHORTS, pols), BF16),
            pltpu.VMEM((pols, lanes), F32),
            pltpu.VMEM((pols, lanes), F32),
            pltpu.VMEM((h, 2, rows, lanes), F32),
            pltpu.VMEM((n, rows, lanes), F32),
            pltpu.VMEM((2, rows, lanes), F32),
            pltpu.VMEM((peers, 2, lanes), F32),
            pltpu.VMEM((2 * peers, 2, lanes), F32),
            dma((2,)),
            dma((2,)),
            dma((2,)),
            dma((2,)),
            dma((h, 2, 2)),
            dma((h, 2)),
            dma((h, 2)),
            dma((n,)),
            dma((1,)),
            dma((1,)),
            dma((peers,)),
            dma((peers,)),
            dma((2 * peers,)),
            dma((2 * peers,)),
        ],
        compiler_params=pltpu.CompilerParams(
            collective_id=0, has_side_effects=True, vmem_limit_bytes=32 * 1024 * 1024
        ),
        cost_estimate=pl.CostEstimate(
            flops=10 * pols * h * lanes * months, bytes_accessed=1 << 20, transcendentals=0
        ),
    )(
        cash_flow,
        fund_units,
        term_months.reshape(1, pols),
        cohort.reshape(1, pols),
        guar_type.reshape(1, pols),
        surrender.reshape(1, pols),
        discount,
        fund_index,
        strike,
    )
    return cohort_pv, tail.reshape(COHORTS)


def solution(mesh):
    return jax.shard_map(
        per_device,
        mesh=mesh,
        in_specs=(
            P("month", ("groups", "blk")),
            P("month", ("groups", "blk")),
            P(("groups", "blk")),
            P(("groups", "blk")),
            P(("groups", "blk")),
            P(("groups", "blk")),
            P(None, ("groups", "blk", "scen")),
            P(None, ("groups", "blk", "scen")),
            P(),
        ),
        out_specs=(P("groups", ("blk", "scen")), P("groups")),
        check_vma=False,
    )
```

time: 122 us -> 43.2 us (0.35)
  waiting for transfers between devices: 47.6 us -> 0 us
  blocking collectives: 44.2 us -> 0 us
  Pallas kernels: 0 us -> 36.2 us
  between operations: 14.2 us -> 0.67 us
  other arithmetic: 7.69 us -> 0 us
  local copies, waits for them, and re-layouts: 2.38 us -> 6.13 us
  starting transfers between devices: 3.51 us -> 0 us
  matrix products: 1.79 us -> 0 us
    psum x3 -> x0, blocking collectives: 40.3 us -> none  [the longest x1 18.6 us: per_device(): lax.psum((jnp.sum(cohort_pv, axis=1), jnp.sum(cohort_pv * cohort_pv, axis...]
    pallas_call x0 -> x1, Pallas kernels: none -> 36.2 us  [per_device(): pl.pallas_call(functools.partial(kernel, n, nx, scaling), out_shape=(jax....]
    all_gather x1 -> x0, waiting for transfers between devices: 29.6 us -> none  [per_device(): pieces = lax.all_gather(scen_pair, 'blk', axis=2, tiled=True)]
    reduce_scatter x1 -> x0, waiting for transfers between devices: 17.6 us -> none  [per_device(): lax.psum_scatter(all_blocks, 'blk', scatter_dimension=1, tiled=True)]
    unnamed x18 -> x20, local copies, waits for them, and re-layouts: 0.79 us -> 6.12 us
    convert_element_type x3 -> x0, other arithmetic: 4.31 us -> none  [the longest x1 4.23 us: make_payoffs(): jnp.maximum(strike[level] - index_f32, 0.0).astype(jnp.bfloat16)]
    all_to_all x1 -> x0, blocking collectives: 3.86 us -> none  [per_device(): lax.all_to_all(fund_units, 'month', split_axis=1, concat_axis=0, tiled=True)]
    all_to_all x1 -> x0, starting transfers between devices: 3.43 us -> none  [per_device(): lax.all_to_all(cash_flow, 'month', split_axis=1, concat_axis=0, tiled=True)]
  transfers between devices with their start and end apart: 3 -> 0, of which waited for: 3 -> 0; matrix products, arithmetic and copies ran while one was open for 2% -> 0% of each run, Pallas kernels for 0% -> 0%
where the time goes in v1:
time: 43.2 us; the launch traced here: 43 us
  Pallas kernels  36.2 us (84%)
  local copies, waits for them, and re-layouts  6.13 us (14%)
  between operations  0.67 us (2%)
    pallas_call x1, Pallas kernels, per_device(): pl.pallas_call(functools.partial(kernel, n, nx, scaling), out_shape=(jax....  36.2 us
    unnamed x20, local copies, waits for them, and re-layouts  6.12 us

profile of v1, /device:TPU:0, one launch (start us, length us, event | category | flops | bytes accessed | tf_op | source)
XLA Modules:
  0.0 43.0 jit_solution(16554481036537065502)
XLA Ops:
  0.6 0.0 copy-start.8
  0.6 0.0 copy-start.5
  0.7 0.0 copy-start.6
  0.7 0.6 %copy-done.8 = bf16[256]{0:T(256)(128)(2,1)S(1)} copy-done((bf16[256]{0:T(256)(128)(2,1)S(1)}, bf16[256]{0:T(256)(128)(2,1)}, u32[]{:S(2)}) %copy-start.8) | copy-done | bytes 536
  1.3 0.0 copy-start.4
  1.3 0.0 copy-start.7
  1.3 0.0 copy-done.5
  1.3 0.0 copy-done.6
  1.3 0.6 %copy-done.4 = s32[256]{0:T(256)S(1)} copy-done((s32[256]{0:T(256)S(1)}, s32[256]{0:T(256)}, u32[]{:S(2)}) %copy-start.4) | copy-done | bytes 1048
  2.0 0.0 copy-done.7
  2.0 0.0 copy-start
  2.0 0.9 %copy-done = bf16[360,256]{1,0:T(8,128)(2,1)S(1)} copy-done((bf16[360,256]{1,0:T(8,128)(2,1)S(1)}, bf16[360,256]{1,0:T(8,128)(2,1)}, u32[]{:S(2)}) %copy-start) | copy-done | bytes 184344
  2.9 0.0 copy-start.1
  2.9 0.9 %copy-done.1 = bf16[360,256]{1,0:T(8,128)(2,1)S(1)} copy-done((bf16[360,256]{1,0:T(8,128)(2,1)S(1)}, bf16[360,256]{1,0:T(8,128)(2,1)}, u32[]{:S(2)}) %copy-start.1) | copy-done | bytes 184344
  3.8 0.0 copy-start.2
  3.8 0.9 %copy-done.2 = bf16[720,128]{1,0:T(8,128)(2,1)S(1)} copy-done((bf16[720,128]{1,0:T(8,128)(2,1)S(1)}, bf16[720,128]{1,0:T(8,128)(2,1)}, u32[]{:S(2)}) %copy-start.2) | copy-done | bytes 184344
  4.7 0.0 copy-start.3
  4.7 0.9 %copy-done.3 = bf16[720,128]{1,0:T(8,128)(2,1)S(1)} copy-done((bf16[720,128]{1,0:T(8,128)(2,1)S(1)}, bf16[720,128]{1,0:T(8,128)(2,1)}, u32[]{:S(2)}) %copy-start.3) | copy-done | bytes 184344
  5.7 36.2 %shard_map.104 = (f32[64,128]{1,0:T(8,128)S(1)}, f32[1,64]{1,0:T(1,128)S(1)}) custom-call(bf16[360,256]{1,0:T(8,128)(2,1)S(1)} %copy-done, bf16[360,256]{1,0:T(8,128)(2,1)S(1)} %copy-done.1, s32[1,256]{1,0:T(1,128)S(1)} %bitcast.4, s32[1,256]{1,0:T(1,128)S(1)} %bitcast.5, s32[1,256]{1,0:T(1,128)S(1)} %bitcast.6, bf16[1,256]{1,0:T(2,128)(2,1)S(1)} %reshape.22.floor_ref, ...), custom_call_target="tpu_custom_call" | custom-call | flops 471859200 | bytes 1048576 | tf_op jit(solution)/shard_map/pallas_call | solution.py:400
  41.8 0.6 %copy.13 = f32[64,128]{1,0:T(8,128)} copy(f32[64,128]{1,0:T(8,128)S(1)} %get-tuple-element.8) | data formatting | bytes 65536
  42.4 0.5 %copy.14 = f32[64]{0:T(128)} copy(f32[64]{0:T(128)S(1)} %bitcast.7) | data formatting | bytes 512
  (1 shorter events, 0.0 us)
Async XLA Ops:
  0.6 0.7 %copy-start.8 = (bf16[256]{0:T(256)(128)(2,1)S(1)}, bf16[256]{0:T(256)(128)(2,1)}, u32[]{:S(2)}) copy-start(bf16[256]{0:T(256)(128)(2,1)} %param.14) | copy-start | bytes 1540
  0.6 0.7 %copy-start.5 = (s32[256]{0:T(256)S(1)}, s32[256]{0:T(256)}, u32[]{:S(2)}) copy-start(s32[256]{0:T(256)} %param.12) | copy-start | bytes 3076
  0.7 0.7 %copy-start.6 = (s32[256]{0:T(256)S(1)}, s32[256]{0:T(256)}, u32[]{:S(2)}) copy-start(s32[256]{0:T(256)} %param.13) | copy-start | bytes 3076
  1.3 0.7 %copy-start.4 = (s32[256]{0:T(256)S(1)}, s32[256]{0:T(256)}, u32[]{:S(2)}) copy-start(s32[256]{0:T(256)} %param.11) | copy-start | bytes 3076
  1.3 0.7 %copy-start.7 = (f32[4]{0:T(128)S(1)}, f32[4]{0:T(128)}, u32[]{:S(2)}) copy-start(f32[4]{0:T(128)} %strike_ref.1) | copy-start | bytes 52
  2.0 0.9 %copy-start = (bf16[360,256]{1,0:T(8,128)(2,1)S(1)}, bf16[360,256]{1,0:T(8,128)(2,1)}, u32[]{:S(2)}) copy-start(bf16[360,256]{1,0:T(8,128)(2,1)} %cash_ref.1) | copy-start | bytes 552964
  2.9 0.9 %copy-start.1 = (bf16[360,256]{1,0:T(8,128)(2,1)S(1)}, bf16[360,256]{1,0:T(8,128)(2,1)}, u32[]{:S(2)}) copy-start(bf16[360,256]{1,0:T(8,128)(2,1)} %fund_ref.1) | copy-start | bytes 552964
  3.8 0.9 %copy-start.2 = (bf16[720,128]{1,0:T(8,128)(2,1)S(1)}, bf16[720,128]{1,0:T(8,128)(2,1)}, u32[]{:S(2)}) copy-start(bf16[720,128]{1,0:T(8,128)(2,1)} %disc_ref.1) | copy-start | bytes 552964
  4.7 0.9 %copy-start.3 = (bf16[720,128]{1,0:T(8,128)(2,1)S(1)}, bf16[720,128]{1,0:T(8,128)(2,1)}, u32[]{:S(2)}) copy-start(bf16[720,128]{1,0:T(8,128)(2,1)} %index_ref.1) | copy-start | bytes 552964

commit v2 on v1

v2 whole, which is shorter than its diff:
```python
import functools
import math

import jax
import jax.numpy as jnp
from jax import lax
from jax.experimental import pallas as pl
from jax.experimental.pallas import tpu as pltpu
from jax.sharding import PartitionSpec as P

COHORTS = 64
MESH = pl.DeviceIdType.MESH
BF16 = jnp.bfloat16
F32 = jnp.float32


def remote(src, dst, send_sem, recv_sem, **where):
    return pltpu.make_async_remote_copy(
        src_ref=src,
        dst_ref=dst,
        send_sem=send_sem,
        recv_sem=recv_sem,
        device_id=where,
        device_id_type=MESH,
    )


def kernel(
    n,
    nx,
    scaling,
    cash_ref,
    fund_ref,
    term_hbm,
    cohort_hbm,
    type_hbm,
    floor_hbm,
    disc_ref,
    index_ref,
    strike_hbm,
    pv_ref,
    tail_ref,
    pol,
    scen,
    lhs,
    hot,
    kind,
    floor,
    part,
    red,
    pv,
    stat,
    tails,
    pol_local,
    pol_send,
    pol_recv,
    own_local,
    scen_send,
    scen_recv,
    red_send,
    red_recv,
    pv_send,
    pv_recv,
    stat_send,
    stat_recv,
    tail_send,
    tail_recv,
    final,
    term_ref,
    cohort_ref,
    type_ref,
    floor_ref,
    strike_ref,
    small_local,
):
    z = lax.axis_index("blk")
    x = lax.axis_index("scen")
    core = lax.axis_index("month")
    other = 1 - core
    h = n // 2
    low = core * h
    half, pols = cash_ref.shape
    months, lanes = disc_ref.shape
    types = strike_hbm.shape[0]
    depth = lhs.shape[2]
    first = -(-months // 32) * 16
    pieces = ((0, first), (first, months - first))
    chunks = [(a, k) for k in range(2) for a in range(2)]
    scen_total = n * nx * lanes
    peers = n * nx
    me = z * nx + x

    barrier = pltpu.get_barrier_semaphore()

    def greet(**where):
        pl.semaphore_signal(barrier, inc=1, device_id=where, device_id_type=MESH)

    greet(month=other)

    @pl.when(core == 0)
    def _():
        @pl.when(z > 0)
        def _():
            greet(blk=z - 1)

        @pl.when(z < n - 1)
        def _():
            greet(blk=z + 1)

    @pl.when(core == 1)
    def _():
        def peer(i, carry):
            to = lax.rem(me + i, peers)
            greet(blk=to // nx, scen=lax.rem(to, nx))
            return carry

        lax.fori_loop(1, peers, peer, 0)

        def line_peer(i, carry):
            greet(blk=lax.rem(z + i, n), month=jnp.int32(0))
            return carry

        lax.fori_loop(1, n, line_peer, 0)

    small = [
        pltpu.make_async_copy(src, dst, small_local.at[k])
        for k, (src, dst) in enumerate(
            (
                (term_hbm, term_ref),
                (cohort_hbm, cohort_ref),
                (type_hbm, type_ref),
                (floor_hbm, floor_ref),
                (strike_hbm, strike_ref),
            )
        )
    ]
    for copy in small:
        copy.start()
    own_pol = [
        pltpu.make_async_copy(ref, pol.at[core, a], pol_local.at[a])
        for a, ref in enumerate((cash_ref, fund_ref))
    ]
    for copy in own_pol:
        copy.start()
    mine = (z >= low) & (z < low + h)

    def own_scen(a):
        ref = (disc_ref, index_ref)[a]
        return pltpu.make_async_copy(ref, scen.at[z - low, a], own_local.at[a])

    @pl.when(mine)
    def _():
        for a in range(2):
            own_scen(a).start()

    around = jnp.where(z > 0, 1, 0) + jnp.where(z < n - 1, 1, 0)
    pl.semaphore_wait(barrier, jnp.where(core == 1, peers, n + around))

    def piece(ref, k):
        return ref.at[pl.ds(pieces[k][0], pieces[k][1])]

    def hop(src, j, a, k, right):
        return remote(
            piece(src, k),
            piece(scen.at[j, a], k),
            scen_send.at[j, a, k, right],
            scen_recv.at[j, a, k],
            blk=z + (1 if right else -1),
        )

    for a, k in chunks:
        ref = (disc_ref, index_ref)[a]

        @pl.when(mine & (z < n - 1))
        def _():
            hop(ref, z - low, a, k, 1).start()

        @pl.when(mine & (z > 0))
        def _():
            hop(ref, z - low, a, k, 0).start()

    give_pol = [
        remote(ref, pol.at[core, a], pol_send.at[a], pol_recv.at[a], month=other)
        for a, ref in enumerate((cash_ref, fund_ref))
    ]
    for copy in give_pol:
        copy.start()

    for copy in small:
        copy.wait()
    term = term_ref[...].reshape(1, pols)
    month = lax.broadcasted_iota(jnp.int32, (depth, pols), 0)
    in_force = month < term
    cohort_row = cohort_ref[...].reshape(1, pols)
    hot[...] = jnp.where(
        lax.broadcasted_iota(jnp.int32, (COHORTS, pols), 0) == cohort_row, 1.0, 0.0
    ).astype(BF16)
    kind[...] = jnp.broadcast_to(type_ref[...].reshape(1, pols).astype(F32), (lanes, pols)).T
    floor[...] = jnp.broadcast_to(floor_ref[...].astype(F32).reshape(1, pols), (lanes, pols)).T
    for a in range(2):
        own_pol[a].wait()
        remote(
            pol.at[other, a], pol.at[other, a], pol_send.at[a], pol_recv.at[a], month=other
        ).wait_recv()
        held = jnp.concatenate(
            [
                pol[0, a].astype(F32),
                pol[1, a].astype(F32),
                jnp.zeros((depth - months, pols), F32),
            ],
            axis=0,
        )
        lhs[a] = jnp.where(in_force, held, 0.0).T.astype(BF16)

    def cohort_terms(j):
        pad = jnp.zeros((depth - months, lanes), BF16)
        disc = jnp.concatenate([scen[j, 0], pad], axis=0)
        net = jnp.dot(lhs[0], disc, preferred_element_type=F32)
        index = scen[j, 1].astype(F32)
        pays = jnp.concatenate(
            [
                jnp.concatenate(
                    [jnp.maximum(strike_ref[t] - index, 0.0).astype(BF16), pad], axis=0
                )
                for t in range(types)
            ],
            axis=1,
        )
        every = jnp.dot(lhs[1], pays, preferred_element_type=F32)
        which = kind[...]
        guarantee = every[:, :lanes]
        for t in range(1, types):
            guarantee = jnp.where(which == t, every[:, t * lanes : (t + 1) * lanes], guarantee)
        value = jnp.maximum(net + guarantee, floor[...])
        high = value.astype(BF16)
        rest = value - high.astype(F32)
        middle = rest.astype(BF16)
        least = (rest - middle.astype(F32)).astype(BF16)
        sums = jnp.dot(
            hot[...], jnp.concatenate([high, middle, least], axis=1), preferred_element_type=F32
        )
        return sums[:, :lanes] + sums[:, lanes : 2 * lanes] + sums[:, 2 * lanes :]

    def give_red(j):
        return remote(
            part.at[j], red.at[z], red_send.at[j], red_recv.at[z], blk=low + j, month=jnp.int32(1)
        )

    def step(t, carry):
        d = (t + 1) // 2
        b = jnp.where(lax.rem(t, 2) == 1, z - d, z + d)
        j = b - low

        @pl.when((j >= 0) & (j < h))
        def _():
            @pl.when(b == z)
            def _():
                for a in range(2):
                    own_scen(a).wait()

            for a, k in chunks:
                @pl.when(b < z)
                def _():
                    hop(scen.at[j, a], j, a, k, 1).wait_recv()

                @pl.when(b > z)
                def _():
                    hop(scen.at[j, a], j, a, k, 0).wait_recv()

                @pl.when((b < z) & (z < n - 1))
                def _():
                    hop(scen.at[j, a], j, a, k, 1).start()

                @pl.when((b > z) & (z > 0))
                def _():
                    hop(scen.at[j, a], j, a, k, 0).start()

            sums = cohort_terms(j)
            part[j] = sums

            @pl.when((b == z) & (core == 1))
            def _():
                red[z] = sums

            @pl.when((b != z) | (core != 1))
            def _():
                give_red(j).start()

        return carry

    lax.fori_loop(0, 2 * n - 1, step, 0)

    give_pv = remote(pv, pv, pv_send.at[0], pv_recv.at[0], month=other)
    give_final = remote(final, final, pv_send.at[1], pv_recv.at[1], month=other)

    def each(first, last, action):
        def go(i, carry):
            action(i)
            return carry

        lax.fori_loop(first, last, go, 0)

    def share(ref, send_sem, recv_sem, i, slot):
        to = lax.rem(me + i, peers)
        where = slot(to)
        return remote(
            ref.at[where],
            ref.at[where],
            send_sem.at[i],
            recv_sem.at[where],
            blk=to // nx,
            scen=lax.rem(to, nx),
        )

    def give(ref, send_sem, recv_sem, i):
        return share(ref, send_sem, recv_sem, i, lambda to: me)

    def take(ref, send_sem, recv_sem, i):
        return share(ref, send_sem, recv_sem, i, lambda to: to)

    @pl.when(core == 1)
    def _():
        owner = z // h

        def take_red(i):
            @pl.when((i != z) | (owner != 1))
            def _():
                remote(red.at[i], red.at[i], red_send.at[0], red_recv.at[i], month=other).wait_recv()

        each(0, n, take_red)
        own = red[0]
        for i in range(1, n):
            own = own + red[i]
        own = own * scaling
        turned = jnp.concatenate([own, jnp.zeros((lanes - COHORTS, lanes), F32)], axis=0).T
        stat[me] = jnp.concatenate(
            [
                jnp.sum(turned, axis=0, keepdims=True),
                jnp.sum(turned * turned, axis=0, keepdims=True),
            ],
            axis=0,
        )
        each(1, peers, lambda i: give(stat, stat_send, stat_recv, i).start())
        pv[...] = own
        give_pv.start()
        pv_ref[...] = own
        each(1, peers, lambda i: take(stat, stat_send, stat_recv, i).wait_recv())
        stats = jnp.sum(stat[...], axis=0)
        centre = stats[0:1] / scen_total
        spread = stats[1:2] / scen_total - centre * centre
        temper = 0.5 * jnp.sqrt(spread + 1e-05)
        weights = jax.nn.sigmoid((turned - centre) / temper)
        tails[me] = jnp.concatenate(
            [
                jnp.sum(weights * turned, axis=0, keepdims=True),
                jnp.sum(weights, axis=0, keepdims=True),
            ],
            axis=0,
        )
        each(1, peers, lambda i: give(tails, tail_send, tail_recv, i).start())
        each(1, peers, lambda i: give(stat, stat_send, stat_recv, i).wait_send())
        give_pv.wait_send()
        each(1, peers, lambda i: take(tails, tail_send, tail_recv, i).wait_recv())
        ends = jnp.sum(tails[...], axis=0)
        final[...] = ends[0:1] / ends[1:2]
        give_final.start()

    for copy in give_pol:
        copy.wait_send()

    def finish(j, carry):
        b = low + j
        for a, k in chunks:
            @pl.when((b <= z) & (z < n - 1))
            def _():
                hop(scen.at[j, a], j, a, k, 1).wait_send()

            @pl.when((b >= z) & (z > 0))
            def _():
                hop(scen.at[j, a], j, a, k, 0).wait_send()

        @pl.when((b != z) | (core != 1))
        def _():
            give_red(j).wait_send()

        return carry

    lax.fori_loop(0, h, finish, 0)

    @pl.when(core == 1)
    def _():
        each(1, peers, lambda i: give(tails, tail_send, tail_recv, i).wait_send())
        give_final.wait_send()

    @pl.when(core == 0)
    def _():
        give_pv.wait_recv()
        pv_ref[...] = pv[...]
        give_final.wait_recv()

    tail_ref[...] = final[:, :COHORTS]


def per_device(
    cash_flow, fund_units, term_months, cohort, guar_type, surrender, discount, fund_index, strike
):
    n, nx = lax.axis_size("blk"), lax.axis_size("scen")
    half, pols = cash_flow.shape
    months, lanes = discount.shape
    h = n // 2
    peers = n * nx
    depth = -(-months // 256) * 256
    scaling = 1.0 / math.sqrt(pols * n / COHORTS)
    vmem = pl.BlockSpec(memory_space=pltpu.VMEM)
    hbm = pl.BlockSpec(memory_space=pltpu.HBM)
    dma = pltpu.SemaphoreType.DMA
    cohort_pv, tail = pl.pallas_call(
        functools.partial(kernel, n, nx, scaling),
        out_shape=(
            jax.ShapeDtypeStruct((COHORTS, lanes), F32),
            jax.ShapeDtypeStruct((1, COHORTS), F32),
        ),
        in_specs=[hbm] * 9,
        out_specs=(vmem, vmem),
        scratch_shapes=[
            pltpu.VMEM((2, 2, half, pols), BF16),
            pltpu.VMEM((h, 2, months, lanes), BF16),
            pltpu.VMEM((2, pols, depth), BF16),
            pltpu.VMEM((COHORTS, pols), BF16),
            pltpu.VMEM((pols, lanes), F32),
            pltpu.VMEM((pols, lanes), F32),
            pltpu.VMEM((h, COHORTS, lanes), F32),
            pltpu.VMEM((n, COHORTS, lanes), F32),
            pltpu.VMEM((COHORTS, lanes), F32),
            pltpu.VMEM((peers, 2, lanes), F32),
            pltpu.VMEM((peers, 2, lanes), F32),
            dma((2,)),
            dma((2,)),
            dma((2,)),
            dma((2,)),
            dma((h, 2, 2, 2)),
            dma((h, 2, 2)),
            dma((h,)),
            dma((n,)),
            dma((2,)),
            dma((2,)),
            dma((peers,)),
            dma((peers,)),
            dma((peers,)),
            dma((peers,)),
            pltpu.VMEM((1, lanes), F32),
            pltpu.VMEM((pols,), jnp.int32),
            pltpu.VMEM((pols,), jnp.int32),
            pltpu.VMEM((pols,), jnp.int32),
            pltpu.VMEM((pols,), BF16),
            pltpu.SMEM((strike.shape[0],), F32),
            dma((5,)),
        ],
        compiler_params=pltpu.CompilerParams(
            collective_id=0, has_side_effects=True, vmem_limit_bytes=56 * 1024 * 1024
        ),
        cost_estimate=pl.CostEstimate(
            flops=10 * pols * h * lanes * months, bytes_accessed=1 << 20, transcendentals=0
        ),
    )(
        cash_flow,
        fund_units,
        term_months,
        cohort,
        guar_type,
        surrender,
        discount,
        fund_index,
        strike,
    )
    return cohort_pv, tail.reshape(COHORTS)


def solution(mesh):
    return jax.shard_map(
        per_device,
        mesh=mesh,
        in_specs=(
            P("month", ("groups", "blk")),
            P("month", ("groups", "blk")),
            P(("groups", "blk")),
            P(("groups", "blk")),
            P(("groups", "blk")),
            P(("groups", "blk")),
            P(None, ("groups", "blk", "scen")),
            P(None, ("groups", "blk", "scen")),
            P(),
        ),
        out_specs=(P("groups", ("blk", "scen")), P("groups")),
        check_vma=False,
    )
```

time: 43.2 us -> 34.8 us (0.81)
  local copies, waits for them, and re-layouts: 6.13 us -> 1.89 us
  Pallas kernels: 36.2 us -> 32.1 us
    unnamed x20 -> x4, local copies, waits for them, and re-layouts: 6.12 us -> 1.89 us
    pallas_call x1, Pallas kernels: 36.2 us -> 32.1 us  [per_device(): pl.pallas_call(functools.partial(kernel, n, nx, scaling), out_shape=(jax....]
where the time goes in v2:
time: 34.8 us; the launch traced here: 34.6 us
  Pallas kernels  32.1 us (92%)
  local copies, waits for them, and re-layouts  1.89 us (5%)
  between operations  0.65 us (2%)
    pallas_call x1, Pallas kernels, per_device(): pl.pallas_call(functools.partial(kernel, n, nx, scaling), out_shape=(jax....  32.1 us
    unnamed x4, local copies, waits for them, and re-layouts  1.89 us

profile of v2, /device:TPU:0, one launch (start us, length us, event | category | flops | bytes accessed | tf_op | source)
XLA Modules:
  0.0 34.6 jit_solution(18047239042219898231)
XLA Ops:
  0.6 32.1 %shard_map.104 = (f32[64,128]{1,0:T(8,128)}, f32[1,64]{1,0:T(1,128)}) custom-call(bf16[360,256]{1,0:T(8,128)(2,1)} %cash_ref.1, bf16[360,256]{1,0:T(8,128)(2,1)} %fund_ref.1, s32[256]{0:T(256)} %term_hbm.1, s32[256]{0:T(256)} %cohort_hbm.1, s32[256]{0:T(256)} %type_hbm.1, bf16[256]{0:T(256)(128)(2,1)} %floor_hbm.1, bf16[720,128]{1,0:T(8,128)(2,1)} %disc_ref.1, ...), custom_call_target="tpu_custom_call" | custom-call | flops 471859200 | bytes 1048576 | tf_op jit(solution)/shard_map/pallas_call | solution.py:417
  32.7 0.0 copy-start
  32.7 1.4 %copy.13 = f32[64,128]{1,0:T(8,128)} copy(f32[64,128]{1,0:T(8,128)} %get-tuple-element.8) | data formatting | bytes 65536
  34.1 0.0 copy-done
  34.1 0.5 %copy.14 = f32[64]{0:T(128)} copy(f32[64]{0:T(128)S(1)} %bitcast.1) | data formatting | bytes 512
Async XLA Ops:
  32.7 1.4 %copy-start = (f32[1,64]{1,0:T(1,128)S(1)}, f32[1,64]{1,0:T(1,128)}, u32[]{:S(2)}) copy-start(f32[1,64]{1,0:T(1,128)} %get-tuple-element.5) | copy-start | bytes 772

commit v3 on v2

--- a/solution.py
+++ b/solution.py
@@ -78,7 +78,8 @@
     core = lax.axis_index("month")
     other = 1 - core
     h = n // 2
-    low = core * h
+    side = z // h
+    low = h * jnp.where(core == 0, side, 1 - side)
     half, pols = cash_ref.shape
     months, lanes = disc_ref.shape
     types = strike_hbm.shape[0]
@@ -166,6 +167,7 @@
             scen_send.at[j, a, k, right],
             scen_recv.at[j, a, k],
             blk=z + (1 if right else -1),
+            month=jnp.where((z + (1 if right else -1)) // h == side, core, 1),
         )
 
     for a, k in chunks:
@@ -278,13 +280,7 @@
             sums = cohort_terms(j)
             part[j] = sums
 
-            @pl.when((b == z) & (core == 1))
-            def _():
-                red[z] = sums
-
-            @pl.when((b != z) | (core != 1))
-            def _():
-                give_red(j).start()
+            give_red(j).start()
 
         return carry
 
@@ -320,12 +316,8 @@
 
     @pl.when(core == 1)
     def _():
-        owner = z // h
-
         def take_red(i):
-            @pl.when((i != z) | (owner != 1))
-            def _():
-                remote(red.at[i], red.at[i], red_send.at[0], red_recv.at[i], month=other).wait_recv()
+            remote(red.at[i], red.at[i], red_send.at[0], red_recv.at[i], month=other).wait_recv()
 
         each(0, n, take_red)
         own = red[0]
@@ -379,9 +371,7 @@
             def _():
                 hop(scen.at[j, a], j, a, k, 0).wait_send()
 
-        @pl.when((b != z) | (core != 1))
-        def _():
-            give_red(j).wait_send()
+        give_red(j).wait_send()
 
         return carry
 

time: 34.8 us -> 34 us (0.977)
  Pallas kernels: 32.1 us -> 31.3 us
    pallas_call x1, Pallas kernels: 32.1 us -> 31.3 us  [per_device(): pl.pallas_call(functools.partial(kernel, n, nx, scaling), out_shape=(jax....]
where the time goes in v3:
time: 34 us; the launch traced here: 33.8 us
  Pallas kernels  31.3 us (92%)
  local copies, waits for them, and re-layouts  1.89 us (6%)
  between operations  0.65 us (2%)
    pallas_call x1, Pallas kernels, per_device(): pl.pallas_call(functools.partial(kernel, n, nx, scaling), out_shape=(jax....  31.3 us
    unnamed x4, local copies, waits for them, and re-layouts  1.89 us

profile of v3, /device:TPU:0, one launch (start us, length us, event | category | flops | bytes accessed | tf_op | source)
XLA Modules:
  0.0 33.8 jit_solution(11841242978081170632)
XLA Ops:
  0.6 31.3 %shard_map.104 = (f32[64,128]{1,0:T(8,128)}, f32[1,64]{1,0:T(1,128)}) custom-call(bf16[360,256]{1,0:T(8,128)(2,1)} %cash_ref.1, bf16[360,256]{1,0:T(8,128)(2,1)} %fund_ref.1, s32[256]{0:T(256)} %term_hbm.1, s32[256]{0:T(256)} %cohort_hbm.1, s32[256]{0:T(256)} %type_hbm.1, bf16[256]{0:T(256)(128)(2,1)} %floor_hbm.1, bf16[720,128]{1,0:T(8,128)(2,1)} %disc_ref.1, ...), custom_call_target="tpu_custom_call" | custom-call | flops 471859200 | bytes 1048576 | tf_op jit(solution)/shard_map/pallas_call | solution.py:407
  31.9 0.0 copy-start
  32.0 1.4 %copy.13 = f32[64,128]{1,0:T(8,128)} copy(f32[64,128]{1,0:T(8,128)} %get-tuple-element.8) | data formatting | bytes 65536
  33.3 0.0 copy-done
  33.3 0.5 %copy.14 = f32[64]{0:T(128)} copy(f32[64]{0:T(128)S(1)} %bitcast.1) | data formatting | bytes 512
Async XLA Ops:
  31.9 1.4 %copy-start = (f32[1,64]{1,0:T(1,128)S(1)}, f32[1,64]{1,0:T(1,128)}, u32[]{:S(2)}) copy-start(f32[1,64]{1,0:T(1,128)} %get-tuple-element.5) | copy-start | bytes 772

commit v4 on v3

--- a/solution.py
+++ b/solution.py
@@ -72,6 +72,7 @@
     floor_ref,
     strike_ref,
     small_local,
+    out_local,
 ):
     z = lax.axis_index("blk")
     x = lax.axis_index("scen")
@@ -286,6 +287,7 @@
 
     lax.fori_loop(0, 2 * n - 1, step, 0)
 
+    out_pv = pltpu.make_async_copy(pv, pv_ref, out_local.at[0])
     give_pv = remote(pv, pv, pv_send.at[0], pv_recv.at[0], month=other)
     give_final = remote(final, final, pv_send.at[1], pv_recv.at[1], month=other)
 
@@ -335,7 +337,7 @@
         each(1, peers, lambda i: give(stat, stat_send, stat_recv, i).start())
         pv[...] = own
         give_pv.start()
-        pv_ref[...] = own
+        out_pv.start()
         each(1, peers, lambda i: take(stat, stat_send, stat_recv, i).wait_recv())
         stats = jnp.sum(stat[...], axis=0)
         centre = stats[0:1] / scen_total
@@ -357,6 +359,11 @@
         final[...] = ends[0:1] / ends[1:2]
         give_final.start()
 
+    @pl.when(core == 0)
+    def _():
+        give_pv.wait_recv()
+        out_pv.start()
+
     for copy in give_pol:
         copy.wait_send()
 
@@ -384,11 +391,10 @@
 
     @pl.when(core == 0)
     def _():
-        give_pv.wait_recv()
-        pv_ref[...] = pv[...]
         give_final.wait_recv()
 
     tail_ref[...] = final[:, :COHORTS]
+    out_pv.wait()
 
 
 def per_device(
@@ -411,7 +417,7 @@
             jax.ShapeDtypeStruct((1, COHORTS), F32),
         ),
         in_specs=[hbm] * 9,
-        out_specs=(vmem, vmem),
+        out_specs=(hbm, vmem),
         scratch_shapes=[
             pltpu.VMEM((2, 2, half, pols), BF16),
             pltpu.VMEM((h, 2, months, lanes), BF16),
@@ -445,6 +451,7 @@
             pltpu.VMEM((pols,), BF16),
             pltpu.SMEM((strike.shape[0],), F32),
             dma((5,)),
+            dma((1,)),
         ],
         compiler_params=pltpu.CompilerParams(
             collective_id=0, has_side_effects=True, vmem_limit_bytes=56 * 1024 * 1024

time: 34 us -> 34 us (level)
  no operation moved by 1% of the time
where the time goes in v4:
time: 34 us; the launch traced here: 33.8 us
  Pallas kernels  31.3 us (92%)
  local copies, waits for them, and re-layouts  1.89 us (6%)
  between operations  0.65 us (2%)
    pallas_call x1, Pallas kernels, per_device(): pl.pallas_call(functools.partial(kernel, n, nx, scaling), out_shape=(jax....  31.3 us
    unnamed x4, local copies, waits for them, and re-layouts  1.89 us

profile of v4, /device:TPU:0, one launch (start us, length us, event | category | flops | bytes accessed | tf_op | source)
XLA Modules:
  0.0 33.8 jit_solution(8769763661426633802)
XLA Ops:
  0.6 31.3 %shard_map.104 = (f32[64,128]{1,0:T(8,128)}, f32[1,64]{1,0:T(1,128)}) custom-call(bf16[360,256]{1,0:T(8,128)(2,1)} %cash_ref.1, bf16[360,256]{1,0:T(8,128)(2,1)} %fund_ref.1, s32[256]{0:T(256)} %term_hbm.1, s32[256]{0:T(256)} %cohort_hbm.1, s32[256]{0:T(256)} %type_hbm.1, bf16[256]{0:T(256)(128)(2,1)} %floor_hbm.1, bf16[720,128]{1,0:T(8,128)(2,1)} %disc_ref.1, ...), custom_call_target="tpu_custom_call" | custom-call | flops 471859200 | bytes 1048576 | tf_op jit(solution)/shard_map/pallas_call | solution.py:413
  31.9 0.0 copy-start
  31.9 1.4 %copy.13 = f32[64,128]{1,0:T(8,128)} copy(f32[64,128]{1,0:T(8,128)} %get-tuple-element.8) | data formatting | bytes 65536
  33.3 0.0 copy-done
  33.3 0.5 %copy.14 = f32[64]{0:T(128)} copy(f32[64]{0:T(128)S(1)} %bitcast.1) | data formatting | bytes 512
Async XLA Ops:
  31.9 1.4 %copy-start = (f32[1,64]{1,0:T(1,128)S(1)}, f32[1,64]{1,0:T(1,128)}, u32[]{:S(2)}) copy-start(f32[1,64]{1,0:T(1,128)} %get-tuple-element.5) | copy-start | bytes 772
